TPU v7x, 32 devices: a whole 2x2x4 slice. The times are simulated.
32 devices in a mesh: gx: 4 (over z), gy: 2 (over y), gz: 4 (over x, core).
Axes of the slice: x: 2, y: 2, z: 4, core: 2. Of those that a mesh axis runs over, the one named last changes fastest.
Arguments:
- tokens: bfloat16 [128, 4096], P(('gy', 'gz'), 'gx'), may hold values from -6 to 6
- expert_ids: int32 [128, 2], P(('gy', 'gz')), may hold values from 0 to 7, all different within a row; in each aligned block of 16 rows (0 to 15, 16 to 31, ...) at most 8 rows name the same one
- gate_probs: float32 [128, 2], P(('gy', 'gz')), may hold values from 0.2 to 1
- gate_weight: bfloat16 [8, 4096, 16384], P('gy', None, ('gz', 'gx')), may hold values from -0.09375 to 0.09375
- up_weight: bfloat16 [8, 4096, 16384], P('gy', None, ('gz', 'gx')), may hold values from -0.09375 to 0.09375
- down_weight: bfloat16 [8, 16384, 4096], P('gy', 'gz', 'gx'), may hold values from -0.046875 to 0.046875
Outputs:
- moe_output: bfloat16 [128, 4096], P(('gy', 'gz'), 'gx')
Inputs may be any that keep to these rules, and one draw needn't show every extreme that they name: `expert_ids`: A token's two ids differ. Within each aligned block of 16 tokens no expert is named more than 8 times, and in some blocks one expert is named exactly 8 times.
All inputs are finite; a program needn't handle non-finite values.
Results may differ from a plain program's by a relative error of at most 0.0049.
Values may be sent and summed in bfloat16 or wider, within the bound.
A program may use at most 192 MiB of HBM per device.

v0:
```python
import jax
import jax.numpy as jnp
from jax import lax
from jax.sharding import PartitionSpec as P

EXPERTS = 8
CAP = 8


def route_tables(expert_ids, gate_probs, experts, capacity):
    token_count = expert_ids.shape[0]
    flattened = expert_ids.reshape(token_count * 2)
    labels = jnp.arange(experts, dtype=jnp.int32)
    onehot = (flattened[:, None] == labels[None, :]).astype(jnp.int32)
    before = jnp.cumsum(onehot, axis=0) - onehot
    slot_index = jnp.sum(before * onehot, axis=1)
    places = flattened * capacity + slot_index
    columns = jnp.arange(experts * capacity, dtype=jnp.int32)
    matches = (places[:, None] == columns[None, :]).astype(jnp.float32)
    matches = matches.reshape(token_count, 2, experts * capacity)
    picker = jnp.sum(matches, axis=1)
    combine_table = jnp.sum(matches * gate_probs[:, :, None], axis=1)
    return (picker, combine_table)


def body(tokens, expert_ids, gate_probs, gate_weight, up_weight, down_weight):
    size_gy = lax.axis_size("gy")
    size_gz = lax.axis_size("gz")
    local_experts = gate_weight.shape[0]
    hidden_cols = gate_weight.shape[2]
    picker, combine_table = route_tables(expert_ids, gate_probs, EXPERTS, CAP)
    selector = picker.astype(jnp.bfloat16)
    full_rows = lax.all_gather(tokens, "gx", axis=1, tiled=True)
    feature_width = full_rows.shape[1]
    buffer = jnp.einsum(
        "tr,tf->rf", selector, full_rows, preferred_element_type=jnp.float32
    ).astype(jnp.bfloat16)
    outgoing = buffer.reshape(size_gy, local_experts, CAP, feature_width).transpose(1, 0, 2, 3)[
        :, :, None
    ]
    arrived = lax.all_to_all(outgoing, "gy", split_axis=1, concat_axis=1, tiled=True)
    portion = lax.all_gather(arrived, "gz", axis=2, tiled=True)
    gate_part = jnp.einsum(
        "jyscd,jdh->jysch", portion, gate_weight, preferred_element_type=jnp.float32
    )
    up_part = jnp.einsum("jyscd,jdh->jysch", portion, up_weight, preferred_element_type=jnp.float32)
    stacked = jnp.concatenate([gate_part, up_part], axis=4)
    gate_act = stacked[..., :hidden_cols].reshape(local_experts, -1, hidden_cols)
    up_act = stacked[..., hidden_cols:].reshape(local_experts, -1, hidden_cols)
    hidden = (jax.nn.silu(gate_act) * up_act).astype(jnp.bfloat16)
    result_width = down_weight.shape[2]
    partial_out = jnp.einsum(
        "jrh,jhf->jrf",
        lax.all_gather(hidden, "gx", axis=2, tiled=True),
        down_weight,
        preferred_element_type=jnp.float32,
    )
    regrouped = partial_out.reshape(local_experts, size_gy * size_gz, CAP, result_width)
    returned = lax.all_to_all(regrouped, ("gy", "gz"), split_axis=1, concat_axis=1, tiled=True)
    results = jnp.sum(returned.reshape(local_experts, size_gy, size_gz, CAP, result_width), axis=2)
    expert_table = results.transpose(1, 0, 2, 3).reshape(EXPERTS * CAP, result_width)
    moe_output = jnp.dot(
        combine_table,
        expert_table,
        precision=lax.Precision.HIGHEST,
        preferred_element_type=jnp.float32,
    )
    return moe_output.astype(jnp.bfloat16)


def solution(mesh):
    return jax.shard_map(
        body,
        mesh=mesh,
        in_specs=(
            P(("gy", "gz"), "gx"),
            P(("gy", "gz"), None),
            P(("gy", "gz"), None),
            P("gy", None, ("gz", "gx")),
            P("gy", None, ("gz", "gx")),
            P("gy", "gz", "gx"),
        ),
        out_specs=P(("gy", "gz"), "gx"),
        check_vma=False,
    )
```

profile of v0, /device:TPU:0, one launch (start us, length us, event | category | flops | bytes accessed | tf_op | source)
XLA Modules:
  0.0 174.2 jit_solution(11500437617051720794)
XLA Ops:
  6.5 0.0 all-gather.3.cloned.1.call-start
  6.5 0.8 copy.33
  7.3 0.1 eq.29
  7.4 0.1 fusion.8
  7.5 0.1 reduce_window_sum.11
  7.5 0.2 select_reduce_fusion.1
  7.7 0.1 reduce_sum.39
  7.8 0.1 copy.34
  7.9 0.7 multiply_add_fusion
  8.6 15.3 %all_gather.9 = bf16[16,4096]{1,0:T(8,128)(2,1)S(1)} all-gather(bf16[16,1024]{1,0:T(8,128)(2,1)} %param.6), channel_id=1, replica_groups=mesh['gx'=4,'gy'=2,'gz'=4] {'gx'}, dimensions={1}, use_global_device_ids=true | all-gather | bytes 163840 | tf_op jit(solution)/shard_map/all_gather | solution.py:33
  23.8 0.8 convert_reduce_fusion
  24.6 0.3 convolution_convert_fusion
  24.9 9.2 %all_to_all.10 = bf16[4,2,1,8,4096]{4,3,2,0,1:T(8,128)(2,1)S(1)} all-to-all(bf16[4,2,1,8,4096]{4,3,2,0,1:T(8,128)(2,1)S(1)} %bitcast.48), channel_id=1, replica_groups=mesh['gx'=4,'gy'=2,'gz'=4] {'gy'}, dimensions={1} | all-to-all | bytes 1048576 | tf_op jit(solution)/shard_map/all_to_all | solution.py:41
  34.1 0.8 copy.35
  34.9 0.0 all-gather.3.cloned.1.call-update
  34.9 0.0 all-gather.5.cloned.1.call-start
  35.0 23.1 %all-gather.3.cloned.1.call-done = bf16[4,2,4,8,4096]{4,3,2,1,0:T(8,128)(2,1)} async-done(((bf16[4,2,1,8,4096]{4,3,2,1,0:T(8,128)(2,1)}), bf16[4,2,4,8,4096]{4,3,2,1,0:T(8,128)(2,1)}) %all-gather.3.cloned.1.call-update) | async-done | bytes 2097168 | tf_op jit(solution)/shard_map/all_gather | solution.py:42
  58.1 0.0 copy-start
  58.1 14.4 %fusion = f32[4,2,4,8,1024]{4,3,2,1,0:T(8,128)S(1)} fusion(bf16[4,2,4,8,4096]{4,3,2,1,0:T(8,128)(2,1)} %all-gather.3.cloned.1.call-done, bf16[4,4096,1024]{2,1,0:T(8,128)(2,1)} %param.10), kind=kOutput, calls=%fused_computation | convolution fusion | flops 2147483648 | bytes 36700160 | tf_op jit(solution)/shard_map/jyscd,jdh->jysch/dot_general | solution.py:46
  72.4 0.0 copy-done
  72.4 13.6 %fusion.2 = f32[4,2,4,8,1024]{4,3,2,1,0:T(8,128)S(1)} fusion(bf16[4,2,4,8,4096]{4,3,2,1,0:T(8,128)(2,1)S(1)} %copy-done, bf16[4,4096,1024]{2,1,0:T(8,128)(2,1)} %param.9), kind=kOutput, calls=%fused_computation.2 | convolution fusion | flops 2147483648 | bytes 36700160 | tf_op jit(solution)/shard_map/jyscd,jdh->jysch/dot_general | solution.py:43
  86.1 1.1 fusion.4
  87.2 0.0 all-gather.5.cloned.1.call-update
  87.2 46.1 %all-gather.5.cloned.1.call-done = bf16[4,64,4096]{2,1,0:T(8,128)(2,1)} async-done(((bf16[4,64,1024]{2,1,0:T(8,128)(2,1)}), bf16[4,64,4096]{2,1,0:T(8,128)(2,1)}) %all-gather.5.cloned.1.call-update) | async-done | bytes 2097168 | tf_op jit(solution)/shard_map/all_gather | solution.py:54
  133.3 14.2 %convolution_bitcast_fusion = f32[4,8,8,1024]{3,2,1,0:T(8,128)S(1)} fusion(bf16[4,64,4096]{2,1,0:T(8,128)(2,1)} %all-gather.5.cloned.1.call-done, bf16[4,4096,1024]{2,1,0:T(8,128)(2,1)} %param.11), kind=kOutput, calls=%fused_computation.5 | convolution fusion | flops 2147483648 | bytes 36700160 | tf_op jit(solution)/shard_map/jrh,jhf->jrf/dot_general | solution.py:52
  147.5 0.1 copy.36
  147.6 18.8 %all_to_all.11 = f32[4,8,8,1024]{3,2,0,1:T(8,128)S(1)} all-to-all(f32[4,8,8,1024]{3,2,0,1:T(8,128)S(1)} %copy.36), channel_id=1, replica_groups=mesh['gx'=4,'gy'=2,'gz'=4] {'gy','gz'}, dimensions={1} | all-to-all | bytes 2097152 | tf_op jit(solution)/shard_map/all_to_all | solution.py:59
  166.4 0.1 bitcast_reduce_fusion
  166.5 0.9 convolution_convert_fusion.1
Async XLA Ops:
  6.5 51.5 %all-gather.3.cloned.1.call-start = ((), (), s32[]{:S(2)}) async-start(), calls=%async_computation.2 | async-start | bytes 2621440 | tf_op jit(solution)/shard_map/all_gather | solution.py:42
  34.9 98.3 %all-gather.5.cloned.1.call-start = ((), (), s32[]{:S(2)}) async-start(), calls=%async_computation.3 | async-start | bytes 2621440 | tf_op jit(solution)/shard_map/all_gather | solution.py:54
  58.1 14.4 %copy-start = (bf16[4,2,4,8,4096]{4,3,2,1,0:T(8,128)(2,1)S(1)}, bf16[4,2,4,8,4096]{4,3,2,1,0:T(8,128)(2,1)}, u32[]{:S(2)}) copy-start(bf16[4,2,4,8,4096]{4,3,2,1,0:T(8,128)(2,1)} %all-gather.3.cloned.1.call-done) | copy-start | bytes 6291460
Sparse Core Ops, SparseCore 0:
  35.1 22.9 all-gather.2
  87.3 45.9 all-gather.4
where the time goes:
time: 174 us
  waiting for transfers between devices  69.2 us (40%)
  matrix products  43.4 us (25%)
  blocking collectives  43.3 us (25%)
  between operations  13.5 us (8%)
  other arithmetic  2.93 us (2%)
  local copies, waits for them, and re-layouts  1.92 us (1%)
    all_gather x1, waiting for transfers between devices, body(): lax.all_gather(hidden, 'gx', axis=2, tiled=True)  46.1 us
    all_gather x1, waiting for transfers between devices, body(): portion = lax.all_gather(arrived, 'gz', axis=2, tiled=True)  23.1 us
    all_to_all x1, blocking collectives, body(): lax.all_to_all(regrouped, ('gy', 'gz'), split_axis=1, concat_axis=1, tile...  18.8 us
    all_gather x1, blocking collectives, body(): full_rows = lax.all_gather(tokens, 'gx', axis=1, tiled=True)  15.3 us
    dot_general x1, matrix products, body(): jnp.einsum('jyscd,jdh->jysch', portion, up_weight, preferred_element_type...  14.4 us
    dot_general x1, matrix products, body(): jnp.einsum('jrh,jhf->jrf', lax.all_gather(hidden, 'gx', axis=2, tiled=Tru...  14.2 us
    dot_general x1, matrix products, body(): jnp.einsum('jyscd,jdh->jysch', portion, gate_weight, preferred_element_ty...  13.6 us
    all_to_all x1, blocking collectives, body(): lax.all_to_all(outgoing, 'gy', split_axis=1, concat_axis=1, tiled=True)  9.16 us
  transfers between devices with their start and end apart: 2, of which 2 were waited for; matrix products, arithmetic and copies ran while one was open for 0% of the time, Pallas kernels for 0%

commit v1 on v0

v1 whole, which is shorter than its diff:
```python
import functools

import jax
import jax.numpy as jnp
from jax import lax
from jax.experimental import pallas as pl
from jax.experimental.pallas import tpu as pltpu
from jax.sharding import PartitionSpec as P

EXPERTS = 8
CAP = 8
MESH = pl.DeviceIdType.MESH
LAG = 2
F32 = jnp.float32
BF16 = jnp.bfloat16


def kernel(
    dims,
    tok_ref,
    info_ref,
    gate_hbm,
    up_hbm,
    down_hbm,
    out_ref,
    ring,
    tokbuf,
    infobuf,
    buf,
    pick,
    pick_t,
    scale,
    hid,
    yhi,
    ylo,
    part,
    parts,
    wsem,
    info_s,
    info_r,
    gx_s,
    gx_r,
    a1_s,
    a1_r,
    a2_s,
    a2_r,
    b1_s,
    b1_r,
    b2_s,
    b2_r,
    core_sem,
    up_s,
    dn_s,
    hid_r,
    out_s,
    out_r,
):
    G, Y, X, C, EL, TOK, W, D, HC, HR, WO, cw, NS = dims
    Z = X * C
    NB = Y * Z
    T = NB * TOK
    R = NB * CAP
    NJ, ND = HC // cw, WO // cw
    U = EL * NJ
    NC = 2 * U + EL * ND
    gx, gy, gz = lax.axis_index("gx"), lax.axis_index("gy"), lax.axis_index("gz")
    cx, cc = gz // C, lax.rem(gz, C)
    block = gy * Z + gz

    def start_gate(u, c):
        j, n = u // NJ, lax.rem(u, NJ)
        cols = pl.ds(pl.multiple_of(n * cw, cw), cw)
        slot = lax.rem(c, NS)
        pltpu.make_async_copy(
            gate_hbm.at[j, :, cols], ring.at[slot, pl.ds(0, D)], wsem.at[slot]
        ).start()

    def start_up(u, c):
        j, n = u // NJ, lax.rem(u, NJ)
        cols = pl.ds(pl.multiple_of(n * cw, cw), cw)
        slot = lax.rem(c, NS)
        pltpu.make_async_copy(
            up_hbm.at[j, :, cols], ring.at[slot, pl.ds(0, D)], wsem.at[slot]
        ).start()

    def start_down(q, c):
        j, n = q // ND, lax.rem(q, ND)
        cols = pl.ds(pl.multiple_of(n * cw, cw), cw)
        slot = lax.rem(c, NS)
        pltpu.make_async_copy(
            down_hbm.at[j, :, cols], ring.at[slot, pl.ds(0, HR)], wsem.at[slot]
        ).start()

    def start_chunk(c):
        gated = c < 2 * U

        @pl.when(jnp.logical_and(gated, lax.rem(c, 2) == 0))
        def _():
            start_gate(c // 2, c)

        @pl.when(jnp.logical_and(gated, lax.rem(c, 2) == 1))
        def _():
            start_up(c // 2, c)

        @pl.when(jnp.logical_and(c >= 2 * U, c < NC))
        def _():
            start_down(c - 2 * U, c)

    def wait_chunk(c, rows):
        slot = lax.rem(c, NS)
        pltpu.make_async_copy(
            ring.at[slot, pl.ds(0, rows)], ring.at[slot, pl.ds(0, rows)], wsem.at[slot]
        ).wait()
        return slot

    lax.fori_loop(0, NS, lambda c, _: (start_chunk(c), 0)[1], 0)

    barrier = pltpu.get_barrier_semaphore()
    for d in range(1, G):
        pl.semaphore_signal(
            barrier, inc=1, device_id={"gx": lax.rem(gx + d, G)}, device_id_type=MESH
        )

    def plane(b):
        return {"gy": b // Z, "gz": lax.rem(b, Z)}

    for d in range(1, NB):
        pl.semaphore_signal(
            barrier, inc=1, device_id=plane(lax.rem(block + d, NB)), device_id_type=MESH
        )
    pl.semaphore_wait(barrier, G - 1 + NB - 1)

    def remote(src, dst, ssem, rsem, device):
        return pltpu.make_async_remote_copy(
            src_ref=src, dst_ref=dst, send_sem=ssem, recv_sem=rsem,
            device_id=device, device_id_type=MESH,
        )

    def ring_copies(n, me, axis_device, src, dst, ssem, rsem):
        copies = []
        for d in range(1, n):
            peer = lax.rem(me + d, n)
            copies.append(remote(src, dst(me), ssem.at[d], rsem.at[me], axis_device(peer)))
        return copies

    def wait_from(n, me, dst, rsem, ssem, axis_device):
        for d in range(1, n):
            peer = lax.rem(me + d, n)
            remote(dst(peer), dst(peer), ssem.at[d], rsem.at[peer], axis_device(peer)).wait_recv()

    on_gx = lambda i: {"gx": i}
    on_gy = lambda i: {"gy": i}
    on_x = lambda i: {"gz": i * C + cc}

    def tok_at(i):
        return tokbuf.at[i, gy, cx, cc]

    gx_copies = ring_copies(G, gx, on_gx, tok_ref, tok_at, gx_s, gx_r)
    for c in gx_copies:
        c.start()

    def info_at(b):
        return infobuf.at[b]

    info_copies = ring_copies(NB, block, plane, info_ref, info_at, info_s, info_r)
    for c in info_copies:
        c.start()
    tokbuf[gx, gy, cx, cc] = tok_ref[...]
    infobuf[block] = info_ref[...]

    H = G // 2
    low, high = pl.ds(0, H), pl.ds(H, G - H)
    wait_from(G, gx, tok_at, gx_r, gx_s, on_gx)

    a1_at = lambda i: tokbuf.at[low, i, cx, cc]
    b1_at = lambda i: tokbuf.at[high, gy, i, cc]
    a2_at = lambda i: tokbuf.at[low, :, i, cc]
    b2_at = lambda i: tokbuf.at[high, i, :, cc]
    a1 = ring_copies(Y, gy, on_gy, a1_at(gy), a1_at, a1_s, a1_r)
    b1 = ring_copies(X, cx, on_x, b1_at(cx), b1_at, b1_s, b1_r)
    for c in a1 + b1:
        c.start()

    wait_from(NB, block, info_at, info_r, info_s, plane)
    info_t = infobuf[...].reshape(T, 128).T
    id0, id1 = info_t[0:1], info_t[1:2]
    p0, p1 = info_t[2:3], info_t[3:4]
    first = (gy * EL).astype(F32)
    chosen = [
        jnp.where(id0 == first + j, 1.0, 0.0) + jnp.where(id1 == first + j, 1.0, 0.0)
        for j in range(EL)
    ]
    padded = chosen + [jnp.zeros((1, T), F32)] * (-EL % 16)
    t2 = lax.broadcasted_iota(jnp.int32, (T, T), 0)
    t1 = lax.broadcasted_iota(jnp.int32, (T, T), 1)
    earlier = jnp.where((t2 < t1) & (t2 // TOK == t1 // TOK), 1.0, 0.0).astype(BF16)
    before = jnp.dot(
        jnp.concatenate(padded, axis=0).astype(BF16), earlier, preferred_element_type=F32
    )
    base = (lax.broadcasted_iota(jnp.int32, (1, T), 1) // TOK * CAP).astype(F32)
    rows = lax.broadcasted_iota(jnp.int32, (R, T), 0).astype(F32)
    tables = []
    for j in range(EL):
        target = jnp.where(chosen[j] > 0.5, base + before[j:j + 1], -1.0)
        table = jnp.where(rows == target, 1.0, 0.0)
        prob = jnp.where(id0 == first + j, p0, p1)
        scale[j * R:(j + 1) * R] = jnp.sum(table * prob, axis=1, keepdims=True)
        tables.append(table)
    table = jnp.concatenate(tables, axis=0)
    pick[...] = table.astype(BF16)
    pick_t[...] = table.T.astype(BF16)

    wait_from(Y, gy, a1_at, a1_r, a1_s, on_gy)
    a2 = ring_copies(X, cx, on_x, a2_at(cx), a2_at, a2_s, a2_r)
    for c in a2:
        c.start()
    wait_from(X, cx, b1_at, b1_r, b1_s, on_x)
    b2 = ring_copies(Y, gy, on_gy, b2_at(gy), b2_at, b2_s, b2_r)
    for c in b2:
        c.start()
    core_copies = []
    for half, (part_g, wait) in enumerate(
        (
            (low, lambda: wait_from(X, cx, a2_at, a2_r, a2_s, on_x)),
            (high, lambda: wait_from(Y, gy, b2_at, b2_r, b2_s, on_gy)),
        )
    ):
        wait()
        other = 1 - cc
        c = remote(
            tokbuf.at[part_g, :, :, cc], tokbuf.at[part_g, :, :, cc],
            core_sem.at[0, half], core_sem.at[1, half], {"gz": cx * C + other},
        )
        c.start()
        core_copies.append(c)
    for half, (c, lo, hi) in enumerate(((core_copies[0], 0, H), (core_copies[1], H, G))):
        c.wait_recv()
        for g in range(lo, hi):
            rows_g = tokbuf[g].reshape(T, W)
            buf[:, g * W:(g + 1) * W] = jnp.dot(
                pick[...], rows_g, preferred_element_type=F32
            ).astype(BF16)

    def hop(u, s, step, sem):
        return remote(
            hid.at[u, s], hid.at[u, s], sem.at[u, s], hid_r.at[u, s],
            {"gx": jnp.clip(gx + step, 0, G - 1)},
        )

    def send_up(u, s):
        @pl.when(gx < G - 1)
        def _():
            hop(u, s, 1, up_s).start()

    def send_down(u, s):
        @pl.when(gx > 0)
        def _():
            hop(u, s, -1, dn_s).start()

    def relay(t):
        for d in range(1, G):
            v = t - LAG * d
            s = gx - d
            live = jnp.logical_and(v >= 0, v < U)

            @pl.when(jnp.logical_and(live, s >= 0))
            def _():
                hop(v, s, -1, dn_s).wait_recv()
                send_up(v, s)

            r = gx + d

            @pl.when(jnp.logical_and(live, r < G))
            def _():
                hop(v, r, 1, up_s).wait_recv()
                send_down(v, r)

    def unit(u):
        j = u // NJ
        x = buf[pl.ds(pl.multiple_of(j * R, R), R), :]
        sg = wait_chunk(2 * u, D)
        gate = jnp.dot(x, ring[sg, pl.ds(0, D), :], preferred_element_type=F32)
        su = wait_chunk(2 * u + 1, D)
        up = jnp.dot(x, ring[su, pl.ds(0, D), :], preferred_element_type=F32)
        hid[u, gx] = (gate / (1.0 + jnp.exp(-gate)) * up).astype(BF16)
        send_up(u, gx)
        send_down(u, gx)
        start_chunk(2 * u + NS)
        start_chunk(2 * u + 1 + NS)

    def step(t, _):
        relay(t)
        unit(t)
        return 0

    lax.fori_loop(0, U, step, 0)

    def down(q):
        j, n = q // ND, lax.rem(q, ND)
        c = 2 * U + q
        slot = wait_chunk(c, HR)
        x = jnp.concatenate(
            [hid[j * NJ + v, s] for s in range(G) for v in range(NJ)], axis=1
        )
        acc = jnp.dot(x, ring[slot, pl.ds(0, HR), :], preferred_element_type=F32)
        start_chunk(c + NS)
        at = pl.ds(pl.multiple_of(j * R, R), R)
        y = acc * scale[at]
        top = y.astype(BF16)
        yhi[n, at] = top
        ylo[n, at] = (y - top.astype(F32)).astype(BF16)

    drain = LAG * (G - 1)
    early = (EL - 1) * ND
    per = -(-early // drain) if early else 0
    fits = all(
        U + q // per >= (q // ND + 1) * NJ - 1 + drain for q in range(early)
    ) if early else True

    def drain_step(i, _):
        relay(U + i)
        for k in range(per if fits else 0):
            q = i * per + k

            @pl.when(q < early)
            def _():
                down(q)

        return 0

    lax.fori_loop(0, drain, drain_step, 0)
    if not fits:
        lax.fori_loop(0, early, lambda q, _: (down(q), 0)[1], 0)

    def give(n, d):
        b = lax.rem(block + d, NB)
        return remote(
            part.at[n, b], parts.at[n, block], out_s.at[n, d], out_r.at[n, block], plane(b)
        )

    def last(n, _):
        down(early + n)
        both = jnp.dot(pick_t[...], yhi[n], preferred_element_type=F32) + jnp.dot(
            pick_t[...], ylo[n], preferred_element_type=F32
        )
        part[n] = both.astype(BF16).reshape(NB, TOK, cw)
        for d in range(1, NB):
            give(n, d).start()
        parts[n, block] = part[n, block]
        return 0

    lax.fori_loop(0, ND, last, 0)

    for n in range(ND):
        for d in range(1, NB):
            b = lax.rem(block + d, NB)
            remote(
                parts.at[n, b], parts.at[n, b], out_s.at[n, d], out_r.at[n, b], plane(b)
            ).wait_recv()
        total = parts[n, 0].astype(F32)
        for b in range(1, NB):
            total = total + parts[n, b].astype(F32)
        out_ref[:, n * cw:(n + 1) * cw] = total.astype(BF16)

    for c in gx_copies + info_copies + a1 + b1 + a2 + b2 + core_copies:
        c.wait_send()

    def settle(u, _):
        for s in range(G):
            @pl.when(jnp.logical_and(gx < G - 1, s <= gx))
            def _():
                hop(u, s, 1, up_s).wait_send()

            @pl.when(jnp.logical_and(gx > 0, s >= gx))
            def _():
                hop(u, s, -1, dn_s).wait_send()

        return 0

    lax.fori_loop(0, U, settle, 0)
    for n in range(ND):
        for d in range(1, NB):
            give(n, d).wait_send()


def body(sizes, tokens, expert_ids, gate_probs, gate_weight, up_weight, down_weight):
    G, Y, Z = sizes
    C = 2
    X = Z // C
    NB = Y * Z
    EL, D, HC = gate_weight.shape
    _, HR, WO = down_weight.shape
    TOK, W = tokens.shape
    cw = min(256, HC, WO)
    T, R = NB * TOK, NB * CAP
    NJ, ND = HC // cw, WO // cw
    U = EL * NJ
    NC = 2 * U + EL * ND
    deep = max(D, HR)
    NS = min(NC, (46 << 20) // (deep * cw * 2)) // 2 * 2
    info = jnp.concatenate(
        [expert_ids.astype(F32), gate_probs, jnp.zeros((TOK, 124), F32)], axis=1
    )
    dims = (G, Y, X, C, EL, TOK, W, D, HC, HR, WO, cw, NS)
    dma = pltpu.SemaphoreType.DMA
    vmem = pl.BlockSpec(memory_space=pltpu.VMEM)
    hbm = pl.BlockSpec(memory_space=pl.ANY)
    return pl.pallas_call(
        functools.partial(kernel, dims),
        out_shape=jax.ShapeDtypeStruct((TOK, WO), BF16),
        in_specs=[vmem, vmem, hbm, hbm, hbm],
        out_specs=vmem,
        scratch_shapes=[
            pltpu.VMEM((NS, deep, cw), BF16),
            pltpu.VMEM((G, Y, X, C, TOK, W), BF16),
            pltpu.VMEM((NB, TOK, 128), F32),
            pltpu.VMEM((EL * R, D), BF16),
            pltpu.VMEM((EL * R, T), BF16),
            pltpu.VMEM((T, EL * R), BF16),
            pltpu.VMEM((EL * R, 1), F32),
            pltpu.VMEM((U, G, R, cw), BF16),
            pltpu.VMEM((ND, EL * R, cw), BF16),
            pltpu.VMEM((ND, EL * R, cw), BF16),
            pltpu.VMEM((ND, NB, TOK, cw), BF16),
            pltpu.VMEM((ND, NB, TOK, cw), BF16),
            dma((NS,)),
            dma((NB,)), dma((NB,)),
            dma((G,)), dma((G,)),
            dma((Y,)), dma((Y,)),
            dma((X,)), dma((X,)),
            dma((X,)), dma((X,)),
            dma((Y,)), dma((Y,)),
            dma((2, 2)),
            dma((U, G)), dma((U, G)), dma((U, G)),
            dma((ND, NB)), dma((ND, NB)),
        ],
        compiler_params=pltpu.CompilerParams(
            collective_id=0, has_side_effects=True, vmem_limit_bytes=60 << 20
        ),
        cost_estimate=pl.CostEstimate(
            flops=2 * EL * R * (2 * D * HC + HR * WO),
            bytes_accessed=2 * EL * (2 * D * HC + HR * WO),
            transcendentals=EL * R * HC,
        ),
    )(tokens, info, gate_weight, up_weight, down_weight)


def solution(mesh):
    sizes = (mesh.shape["gx"], mesh.shape["gy"], mesh.shape["gz"])
    return jax.shard_map(
        functools.partial(body, sizes),
        mesh=mesh,
        in_specs=(
            P(("gy", "gz"), "gx"),
            P(("gy", "gz"), None),
            P(("gy", "gz"), None),
            P("gy", None, ("gz", "gx")),
            P("gy", None, ("gz", "gx")),
            P("gy", "gz", "gx"),
        ),
        out_specs=P(("gy", "gz"), "gx"),
        check_vma=False,
    )
```

time: 174 us -> 79.6 us (0.46)
  Pallas kernels: 0 us -> 75.7 us
  waiting for transfers between devices: 69.2 us -> 0 us
  matrix products: 43.4 us -> 0 us
  blocking collectives: 43.3 us -> 0 us
  between operations: 13.5 us -> 0.01 us
    pallas_call x0 -> x1, Pallas kernels: none -> 75.7 us  [body(): pl.pallas_call(functools.partial(kernel, dims), out_shape=jax.ShapeDtypeS...]
    all_gather x2 -> x0, waiting for transfers between devices: 69.2 us -> none  [the longest x1 46.1 us: body(): lax.all_gather(hidden, 'gx', axis=2, tiled=True)]
    dot_general x5 -> x0, matrix products: 43.4 us -> none  [the longest x1 14.4 us: body(): jnp.einsum('jyscd,jdh->jysch', portion, up_weight, preferred_element_type...]
    all_to_all x2 -> x0, blocking collectives: 28 us -> none  [the longest x1 18.8 us: body(): lax.all_to_all(regrouped, ('gy', 'gz'), split_axis=1, concat_axis=1, tile...]
    all_gather x1 -> x0, blocking collectives: 15.3 us -> none  [body(): full_rows = lax.all_gather(tokens, 'gx', axis=1, tiled=True)]
  transfers between devices with their start and end apart: 2 -> 0, of which waited for: 2 -> 0; matrix products, arithmetic and copies ran while one was open for 0% -> 0% of each run, Pallas kernels for 0% -> 0%
where the time goes in v1:
time: 79.6 us; the launch traced here: 79.3 us
  Pallas kernels  75.7 us (95%)
  local copies, waits for them, and re-layouts  2.29 us (3%)
  other arithmetic  1.36 us (2%)
    pallas_call x1, Pallas kernels, body(): pl.pallas_call(functools.partial(kernel, dims), out_shape=jax.ShapeDtypeS...  75.7 us
    unnamed x2, local copies, waits for them, and re-layouts  2.13 us

profile of v1, /device:TPU:0, one launch (start us, length us, event | category | flops | bytes accessed | tf_op | source)
XLA Modules:
  0.0 79.3 jit_solution(18027551582273921521)
XLA Ops:
  0.0 0.1 pad.2.clone
  0.1 0.7 convert_element_type.3
  0.8 0.1 copy.7
  0.8 0.8 copy.8
  1.6 0.7 maximum_maximum_fusion.info_ref
  2.3 75.7 %shard_map.64 = bf16[16,1024]{1,0:T(8,128)(2,1)} custom-call(bf16[16,1024]{1,0:T(8,128)(2,1)} %tok_ref.1, f32[16,128]{1,0:T(8,128)} %maximum_maximum_fusion.info_ref, bf16[4,4096,1024]{2,1,0:T(8,128)(2,1)} %gate_hbm.1, bf16[4,4096,1024]{2,1,0:T(8,128)(2,1)} %up_hbm.1, bf16[4,4096,1024]{2,1,0:T(8,128)(2,1)} %down_hbm.1), custom_call_target="tpu_custom_call" | custom-call | flops 6442450944 | bytes 100663296 | tf_op jit(solution)/shard_map/pallas_call | solution.py:408
  77.9 1.4 %copy.10 = bf16[16,1024]{1,0:T(8,128)(2,1)} copy(bf16[16,1024]{1,0:T(8,128)(2,1)} %shard_map.64) | data formatting | bytes 65536
  (1 shorter events, 0.0 us)

commit v2 on v1

--- a/solution.py
+++ b/solution.py
@@ -10,7 +10,7 @@
 EXPERTS = 8
 CAP = 8
 MESH = pl.DeviceIdType.MESH
-LAG = 2
+LAG = 3
 F32 = jnp.float32
 BF16 = jnp.bfloat16
 
@@ -184,7 +184,6 @@
     wait_from(NB, block, info_at, info_r, info_s, plane)
     info_t = infobuf[...].reshape(T, 128).T
     id0, id1 = info_t[0:1], info_t[1:2]
-    p0, p1 = info_t[2:3], info_t[3:4]
     first = (gy * EL).astype(F32)
     chosen = [
         jnp.where(id0 == first + j, 1.0, 0.0) + jnp.where(id1 == first + j, 1.0, 0.0)
@@ -203,12 +202,8 @@
     for j in range(EL):
         target = jnp.where(chosen[j] > 0.5, base + before[j:j + 1], -1.0)
         table = jnp.where(rows == target, 1.0, 0.0)
-        prob = jnp.where(id0 == first + j, p0, p1)
-        scale[j * R:(j + 1) * R] = jnp.sum(table * prob, axis=1, keepdims=True)
         tables.append(table)
-    table = jnp.concatenate(tables, axis=0)
-    pick[...] = table.astype(BF16)
-    pick_t[...] = table.T.astype(BF16)
+    pick[...] = jnp.concatenate(tables, axis=0).astype(BF16)
 
     wait_from(Y, gy, a1_at, a1_r, a1_s, on_gy)
     a2 = ring_copies(X, cx, on_x, a2_at(cx), a2_at, a2_s, a2_r)
@@ -233,12 +228,14 @@
         )
         c.start()
         core_copies.append(c)
-    for half, (c, lo, hi) in enumerate(((core_copies[0], 0, H), (core_copies[1], H, G))):
+    for c in core_copies:
         c.wait_recv()
-        for g in range(lo, hi):
-            rows_g = tokbuf[g].reshape(T, W)
-            buf[:, g * W:(g + 1) * W] = jnp.dot(
-                pick[...], rows_g, preferred_element_type=F32
+
+    def fill(j):
+        at = pl.ds(pl.multiple_of(j * R, R), R)
+        for g in range(G):
+            buf[at, g * W:(g + 1) * W] = jnp.dot(
+                pick[at], tokbuf[g].reshape(T, W), preferred_element_type=F32
             ).astype(BF16)
 
     def hop(u, s, step, sem):
@@ -277,6 +274,11 @@
 
     def unit(u):
         j = u // NJ
+
+        @pl.when(lax.rem(u, NJ) == 0)
+        def _():
+            fill(j)
+
         x = buf[pl.ds(pl.multiple_of(j * R, R), R), :]
         sg = wait_chunk(2 * u, D)
         gate = jnp.dot(x, ring[sg, pl.ds(0, D), :], preferred_element_type=F32)
@@ -294,6 +296,14 @@
         return 0
 
     lax.fori_loop(0, U, step, 0)
+
+    pick_t[...] = pick[...].astype(F32).T.astype(BF16)
+    probs_t = infobuf[...].reshape(T, 128).T
+    for j in range(EL):
+        prob = jnp.where(probs_t[0:1] == first + j, probs_t[2:3], probs_t[3:4])
+        scale[j * R:(j + 1) * R] = jnp.sum(
+            pick[j * R:(j + 1) * R].astype(F32) * prob, axis=1, keepdims=True
+        )
 
     def down(q):
         j, n = q // ND, lax.rem(q, ND)

time: 79.6 us -> 72.9 us (0.916)
  Pallas kernels: 75.7 us -> 69 us
    pallas_call x1, Pallas kernels: 75.7 us -> 69 us  [body(): pl.pallas_call(functools.partial(kernel, dims), out_shape=jax.ShapeDtypeS...]
where the time goes in v2:
time: 72.9 us; the launch traced here: 72.7 us
  Pallas kernels  69 us (95%)
  local copies, waits for them, and re-layouts  2.29 us (3%)
  other arithmetic  1.36 us (2%)
    pallas_call x1, Pallas kernels, body(): pl.pallas_call(functools.partial(kernel, dims), out_shape=jax.ShapeDtypeS...  69 us
    unnamed x2, local copies, waits for them, and re-layouts  2.13 us

profile of v2, /device:TPU:0, one launch (start us, length us, event | category | flops | bytes accessed | tf_op | source)
XLA Modules:
  0.0 72.7 jit_solution(2772274789467349756)
XLA Ops:
  0.0 0.1 pad.2.clone
  0.1 0.7 convert_element_type.3
  0.8 0.1 copy.7
  0.8 0.8 %copy.8 = f32[16,2]{1,0:T(8,128)S(1)} copy(f32[16,2]{0,1:T(2,128)} %param.8) | data formatting | bytes 256 | tf_op args[2]
  1.6 0.7 maximum_maximum_fusion.info_ref
  2.3 69.0 %shard_map.64 = bf16[16,1024]{1,0:T(8,128)(2,1)} custom-call(bf16[16,1024]{1,0:T(8,128)(2,1)} %tok_ref.1, f32[16,128]{1,0:T(8,128)} %maximum_maximum_fusion.info_ref, bf16[4,4096,1024]{2,1,0:T(8,128)(2,1)} %gate_hbm.1, bf16[4,4096,1024]{2,1,0:T(8,128)(2,1)} %up_hbm.1, bf16[4,4096,1024]{2,1,0:T(8,128)(2,1)} %down_hbm.1), custom_call_target="tpu_custom_call" | custom-call | flops 6442450944 | bytes 100663296 | tf_op jit(solution)/shard_map/pallas_call | solution.py:418
  71.3 1.4 %copy.10 = bf16[16,1024]{1,0:T(8,128)(2,1)} copy(bf16[16,1024]{1,0:T(8,128)(2,1)} %shard_map.64) | data formatting | bytes 65536
  (1 shorter events, 0.0 us)
